TPU v7x, 32 devices: a whole 2x2x4 slice. The times are simulated.
32 devices in a mesh: groups: 2 (over y), inst: 4 (over z), tp: 4 (over x, core).
Axes of the slice: x: 2, y: 2, z: 4, core: 2. Of those that a mesh axis runs over, the one named last changes fastest.
Arguments:
- kv_pool: bfloat16 [512, 2, 8, 32, 128], P(('groups', 'inst'), None, 'tp'), parts along dimension 0, may hold values from -6 to 6
- page_table: int32 [128, 4], P(('groups', 'inst')), parts along dimension 0, may hold values from 0 to 63, as said below
- lengths: int32 [128], P(('groups', 'inst')), parts along dimension 0, may hold values from 1 to 126
- partner: int32 [128], P(('groups', 'inst')), parts along dimension 0, may hold values from 0 to 63, as said below
- queries: bfloat16 [128, 2, 32, 128], P(('groups', 'inst'), None, 'tp'), parts along dimension 0, may hold values from -150 to 150
- new_kv: bfloat16 [128, 2, 2, 8, 128], P(('groups', 'inst'), None, None, 'tp'), parts along dimension 0, may hold values from -6 to 6
- out_weight: bfloat16 [4096, 2560], P('tp'), may hold values from -0.25 to 0.25
Outputs:
- layer_out: bfloat16 [128, 2, 2560], P(('groups', 'inst', 'tp')), parts along dimension 0
- new_cache: bfloat16 [128, 2, 8, 128, 128], P(('groups', 'inst'), None, 'tp'), parts along dimension 0
There are 2 independent parts, one for each index of `groups`. A program takes and returns all parts, laid end to end along the dimension named above; an argument that names none is the same for every part. Nothing has to cross between parts.
Inputs may be any that keep to these rules, and one draw needn't show every extreme that they name: `page_table`: each instance's rows name distinct pages of its own pool of 64; only the first ceil(lengths / 32) entries of a row are read. Requests trade slots in pairs: partner is its own inverse. At most one request goes from one instance to another.
All inputs are finite; a program needn't handle non-finite values.
Results may differ from a plain program's by a relative error of at most 0.0059.
Values may be sent and summed in bfloat16 or wider, within the bound.
A program may use at most 64 MiB of HBM per device.

v0:
```python
import jax
import jax.numpy as jnp
from jax import lax
from jax.sharding import PartitionSpec as P


def gather_local(kv_pool, page_table, lengths):
    page_rows = kv_pool[page_table]
    r, m, c, g, p, d = page_rows.shape
    stored = page_rows.transpose(0, 2, 3, 1, 4, 5).reshape(r, c, g, m * p, d)
    position = jnp.arange(m * p, dtype=jnp.int32)
    inside = position[None, :] < lengths[:, None]
    return jnp.where(inside[:, None, None, :, None], stored, jnp.zeros((), stored.dtype))


def append_tokens(stored, known_len, fresh):
    position = jnp.arange(stored.shape[3], dtype=jnp.int32)
    for step in range(fresh.shape[1]):
        landing = position[None, :] == (known_len + step)[:, None]
        stored = jnp.where(
            landing[:, None, None, :, None], fresh[:, step][:, :, :, None, :], stored
        )
    return stored


def attend(stored, known_len, asked):
    r, t, h, d = asked.shape
    g = stored.shape[2]
    span = stored.shape[3]
    grouped = asked.reshape(r, t, g, h // g, d)
    scores = jnp.einsum(
        "ntgqd,ngpd->ntgqp", grouped, stored[:, 0], preferred_element_type=jnp.float32
    ) * d ** (-0.5)
    position = jnp.arange(span, dtype=jnp.int32)
    limit = known_len[:, None] + jnp.arange(t, dtype=jnp.int32)[None, :] + 1
    visible = position[None, None, :] < limit[:, :, None]
    scores = jnp.where(visible[:, :, None, None, :], scores, jnp.float32(-1e30))
    largest = jnp.max(scores, axis=-1, keepdims=True)
    expo = jnp.exp(scores - largest)
    weights = (expo / jnp.sum(expo, axis=-1, keepdims=True)).astype(jnp.bfloat16)
    result = jnp.einsum(
        "ntgqp,ngpd->ntgqd", weights, stored[:, 1], preferred_element_type=jnp.float32
    )
    return result.astype(jnp.bfloat16).reshape(r, t, h * d)


def pick_rows(chosen, present, source):
    shaped = present.reshape(present.shape + (1,) * (source.ndim - 1))
    return jnp.where(shaped, source[chosen], jnp.zeros((), source.dtype))


def body(kv_pool, page_table, lengths, partner, queries, new_kv, out_weight):
    slots = lengths.shape[0]
    instances = lax.axis_size("inst")
    current = lax.axis_index("inst")
    mine = gather_local(kv_pool, page_table, lengths)
    partner_inst = partner // slots
    partner_slot = partner % slots
    staying = partner_inst == current
    others = jnp.arange(instances, dtype=jnp.int32)
    slot_ids = jnp.arange(slots, dtype=jnp.int32)
    leaving = (partner_inst[None, :] == others[:, None]) & jnp.logical_not(staying)[None, :]
    present = jnp.any(leaving, axis=1)
    chosen = jnp.sum(jnp.where(leaving, slot_ids[None, :], 0), axis=1)
    outbox = pick_rows(chosen, present, mine)
    out_len = jnp.where(present, lengths[chosen], 0)
    arrived, arrived_len = (
        lax.all_to_all(outbox, "inst", split_axis=0, concat_axis=0, tiled=True),
        lax.all_to_all(
            out_len.astype(jnp.bfloat16), "inst", split_axis=0, concat_axis=0, tiled=True
        ),
    )
    arrived_len = arrived_len.astype(jnp.int32)
    home = mine[partner_slot]
    home_len = lengths[partner_slot]
    holding = jnp.where(staying[:, None, None, None, None], home, arrived[partner_inst])
    holding_len = jnp.where(staying, home_len, arrived_len[partner_inst])
    new_cache = append_tokens(holding, holding_len, new_kv)
    attended = attend(new_cache, holding_len, queries)
    step_count = queries.shape[1]
    features = out_weight.shape[1]
    own_rows = slots // lax.axis_size("tp")
    flattened = attended.reshape(lax.axis_size("tp") * own_rows * step_count, attended.shape[2])
    product = jnp.dot(flattened, out_weight, preferred_element_type=jnp.float32)
    layer_out = lax.psum_scatter(
        product.reshape(lax.axis_size("tp") * own_rows, step_count, features),
        "tp",
        scatter_dimension=0,
        tiled=True,
    ).astype(jnp.bfloat16)
    return (layer_out, new_cache)


def solution(mesh):
    in_specs = (
        P(("groups", "inst"), None, "tp", None, None),
        P(("groups", "inst"), None),
        P(("groups", "inst")),
        P(("groups", "inst")),
        P(("groups", "inst"), None, "tp", None),
        P(("groups", "inst"), None, None, "tp", None),
        P("tp", None),
    )
    out_specs = (
        P(("groups", "inst", "tp"), None, None),
        P(("groups", "inst"), None, "tp", None, None),
    )
    return jax.shard_map(body, mesh=mesh, in_specs=in_specs, out_specs=out_specs, check_vma=False)
```

profile of v0, /device:TPU:0, one launch (start us, length us, event | category | flops | bytes accessed | tf_op | source)
XLA Modules:
  0.0 74.6 jit_solution(7164548983791138322)
XLA Ops:
  0.6 0.8 %compare_select_fusion.1 = (s32[16]{0:T(128)S(1)}, s32[16]{0:T(128)S(1)}, s32[16]{0:T(128)S(1)}) fusion(s32[16]{0:T(128)} %param.10), kind=kLoop, calls=%fused_computation.40 | loop fusion | flops 400 | bytes 256 | tf_op jit(solution)/shard_map/select_n | solution.py:77
  1.5 0.1 select_reduce_fusion
  1.6 0.1 fusion.13
  1.7 1.3 %gather_fusion.1 = s32[4]{0:T(128)S(1)} fusion(s32[16]{0:T(128)} %param.9, s32[1024]{0:T(1024)S(1)} %pad_clamp_fusion.2), kind=kCustom, calls=%fused_computation.1 | custom fusion | bytes 48 | tf_op jit(solution)/shard_map/gather | solution.py:66
  3.0 0.7 copy.56
  3.7 6.3 %all-to-all-start = ((bf16[4,1,1]{2,1,0:T(2,128)(2,1)}), bf16[4,1,1]{2,1,0:T(2,128)(2,1)S(1)}, u32[]{:S(2)}, u32[]{:S(2)}) async-start(bf16[4,1,1]{2,1,0:T(2,128)(2,1)} %copy.56), calls=%async_computation | async-start | bytes 4096 | tf_op jit(solution)/shard_map/all_to_all | solution.py:69
  10.0 0.7 iota_compare_fusion.1
  10.8 1.3 %gather_fusion = s32[16]{0:T(128)S(1)} fusion(s32[16]{0:T(128)} %param.9, s32[1024]{0:T(1024)S(1)} %get-tuple-element.24), kind=kCustom, calls=%fused_computation | custom fusion | bytes 192 | tf_op jit(solution)/shard_map/gather | solution.py:75
  12.1 0.7 compare_select_fusion
  12.9 0.1 reshape.168
  13.0 2.1 %gather_fusion.3 = bf16[64,2,2,32,128]{4,3,2,1,0:T(8,128)(2,1)} fusion(bf16[64,2,2,32,128]{4,3,2,1,0:T(8,128)(2,1)S(1)} %copy-done, s32[1024]{0:T(1024)S(1)} %pad_clamp_fusion), kind=kCustom, calls=%fused_computation.3 | custom fusion | bytes 4194560 | tf_op jit(solution)/shard_map/gather | solution.py:8
  15.1 2.1 %copy.60 = bf16[16,2,2,4,32,128]{5,4,3,2,1,0:T(8,128)(2,1)S(1)} copy(bf16[16,2,2,4,32,128]{5,4,2,1,3,0:T(8,128)(2,1)} %bitcast.43) | data formatting | bytes 4194304 | tf_op jit(solution)/shard_map/transpose | solution.py:10
  17.3 1.7 %bitcast_select_fusion = bf16[16,2,2,128,128]{4,3,2,1,0:T(8,128)(2,1)} fusion(bf16[16,2,2,4,32,128]{5,4,3,2,1,0:T(8,128)(2,1)S(1)} %copy.60, pred[16,128]{1,0:T(8,128)(4,1)S(1)} %iota_compare_fusion.1), kind=kLoop, calls=%fused_computation.10 | loop fusion | flops 1048576 | bytes 4196352 | tf_op jit(solution)/shard_map/jit(_where)/select_n | solution.py:13
  18.9 2.2 %gather_fusion.5 = bf16[4,2,2,128,128]{4,3,2,1,0:T(8,128)(2,1)S(1)} fusion(bf16[16,2,2,128,128]{4,3,2,1,0:T(8,128)(2,1)} %bitcast_select_fusion, s32[1024]{0:T(1024)S(1)} %pad_clamp_fusion.2), kind=kCustom, calls=%fused_computation.5 | custom fusion | bytes 1048592 | tf_op jit(solution)/shard_map/gather | solution.py:49
  21.2 3.8 %gather_fusion.4 = bf16[16,2,2,128,128]{4,3,2,1,0:T(8,128)(2,1)} fusion(bf16[16,2,2,128,128]{4,3,2,1,0:T(8,128)(2,1)} %bitcast_select_fusion, s32[1024]{0:T(1024)S(1)} %get-tuple-element.24), kind=kCustom, calls=%fused_computation.4 | custom fusion | bytes 4194368 | tf_op jit(solution)/shard_map/gather | solution.py:74
  25.0 0.9 %broadcast_select_fusion = bf16[4,2,2,128,128]{4,3,2,1,0:T(8,128)(2,1)} fusion(bf16[4,2,2,128,128]{4,3,2,1,0:T(8,128)(2,1)S(1)} %gather_fusion.5, pred[4]{0:T(512)(128)(4,1)S(1)} %fusion.13), kind=kLoop, calls=%fused_computation.23 | loop fusion | flops 262144 | bytes 1048580 | tf_op jit(solution)/shard_map/jit(_where)/select_n | solution.py:49
  25.9 0.6 dynamic-slice
  27.2 5.1 %all-to-all-start.1 = ((bf16[4,2,2,128,128]{4,3,2,1,0:T(8,128)(2,1)}), bf16[4,2,2,128,128]{4,3,2,1,0:T(8,128)(2,1)S(1)}, u32[]{:S(2)}, u32[]{:S(2)}) async-start(bf16[4,2,2,128,128]{4,3,2,1,0:T(8,128)(2,1)} %broadcast_select_fusion), calls=%async_computation.1 | async-start | bytes 1048576 | tf_op jit(solution)/shard_map/all_to_all | solution.py:68
  32.3 0.2 convert_reduce_fusion
  32.4 0.7 gather_fusion.2
  33.3 0.1 iota_compare_fusion
  33.4 12.8 %all-to-all-done.1 = bf16[4,2,2,128,128]{4,3,2,1,0:T(8,128)(2,1)S(1)} async-done(((bf16[4,2,2,128,128]{4,3,2,1,0:T(8,128)(2,1)}), bf16[4,2,2,128,128]{4,3,2,1,0:T(8,128)(2,1)S(1)}, u32[]{:S(2)}, u32[]{:S(2)}) %all-to-all-start.1) | async-done | bytes 524320 | tf_op jit(solution)/shard_map/all_to_all | solution.py:68
  46.2 2.1 %gather_fusion.6 = bf16[16,2,2,128,128]{4,3,2,1,0:T(8,128)(2,1)} fusion(bf16[4,2,2,128,128]{4,3,2,1,0:T(8,128)(2,1)S(1)} %all-to-all-done.1, s32[1024]{0:T(1024)S(1)} %get-tuple-element.23), kind=kCustom, calls=%fused_computation.6 | custom fusion | bytes 4194368 | tf_op jit(solution)/shard_map/gather | solution.py:76
  48.3 3.5 %fusion.4 = bf16[16,2,2,128,128]{4,3,2,0,1:T(8,128)(2,1)S(1)} fusion(bf16[16,2,2,128,128]{4,3,2,1,0:T(8,128)(2,1)} %gather_fusion.6, bf16[16,2,2,128,128]{4,3,2,1,0:T(8,128)(2,1)} %gather_fusion.4, pred[16]{0:T(512)(128)(4,1)S(1)} %get-tuple-element.19, pred[16,128]{1,0:T(8,128)(4,1)S(1)} %iota_compare_fusion.2, pred[16,128]{1,0:T(8,128)(4,1)S(1)} %iota_compare_fusion.3, ...), kind=kLoop, calls=%fused_computation.13 | loop fusion | flops 3145728 | bytes 6328336 | tf_op jit(solution)/shard_map/jit(_where)/select_n | solution.py:20
  51.8 1.6 %copy.66 = bf16[16,2,2,128,128]{4,3,2,1,0:T(8,128)(2,1)} copy(bf16[16,2,2,128,128]{4,3,2,0,1:T(8,128)(2,1)S(1)} %fusion.4) | data formatting | bytes 4194304
  53.4 0.4 copy-done.1
  53.8 0.6 fusion.8
  54.5 0.3 fusion.16
  54.7 2.2 %fusion.9 = bf16[16,2,2,4,128]{4,3,1,2,0:T(4,128)(2,1)S(1)} fusion(bf16[16,2,2,128,128]{4,3,2,0,1:T(8,128)(2,1)} %copy-done.1, f32[16,2,2,4]{3,1,2,0:T(2,128)S(1)} %fusion.16, f32[16,2,2,4,128]{4,3,1,2,0:T(4,128)S(1)} %fusion.8), kind=kOutput, calls=%fused_computation.20 | convolution fusion | flops 8520063 | bytes 1409024 | tf_op jit(solution)/shard_map/ntgqp,ngpd->ntgqd/dot_general | solution.py:41
  57.0 3.5 %fusion.1 = f32[16,2,2560]{2,0,1:T(8,128)S(1)} fusion(bf16[16,2,1024]{2,0,1:T(8,128)(2,1)S(1)} %dot_general.13, bf16[1024,2560]{1,0:T(8,128)(2,1)} %param.13), kind=kOutput, calls=%fused_computation.8 | convolution fusion | flops 167772160 | bytes 5636096 | tf_op jit(solution)/shard_map/dot_general | solution.py:84
  60.5 13.5 %all-reduce.2 = bf16[16,2,2560]{2,0,1:T(8,128)(2,1)S(1)} all-reduce(f32[16,2,2560]{2,0,1:T(8,128)S(1)} %fusion.1), channel_id=2, replica_groups=mesh['groups'=2,'inst'=4,'tp'=4] {'tp'}, use_global_device_ids=true, to_apply=%region_4.5.clone | all-reduce | flops 81920 | bytes 491520
  74.0 0.6 copy.65
  (25 shorter events, 0.5 us)
Async XLA Ops:
  0.6 12.3 %copy-start = (bf16[64,2,2,32,128]{4,3,2,1,0:T(8,128)(2,1)S(1)}, bf16[64,2,2,32,128]{4,3,2,1,0:T(8,128)(2,1)}, u32[]{:S(2)}) copy-start(bf16[64,2,2,32,128]{4,3,2,1,0:T(8,128)(2,1)} %param.7) | copy-start | bytes 6291460
  3.7 23.4 %all-to-all-start = ((bf16[4,1,1]{2,1,0:T(2,128)(2,1)}), bf16[4,1,1]{2,1,0:T(2,128)(2,1)S(1)}, u32[]{:S(2)}, u32[]{:S(2)}) async-start(bf16[4,1,1]{2,1,0:T(2,128)(2,1)} %copy.56), calls=%async_computation | async-start | bytes 4096 | tf_op jit(solution)/shard_map/all_to_all | solution.py:69
  21.2 4.7 %copy-start.2 = (bf16[16,2,2,2,128]{4,3,2,1,0:T(2,128)(2,1)S(1)}, bf16[16,2,2,2,128]{4,3,2,1,0:T(2,128)(2,1)}, u32[]{:S(2)}) copy-start(bf16[16,2,2,2,128]{4,3,2,1,0:T(2,128)(2,1)} %param.12) | copy-start | bytes 98308
  21.2 4.7 %copy-start.4 = (u32[32]{0:T(128)S(1)}, u32[32]{0:T(128)}, u32[]{:S(2)}) copy-start(u32[32]{0:T(128)} %constant.60) | copy-start | bytes 388
  27.2 19.0 %all-to-all-start.1 = ((bf16[4,2,2,128,128]{4,3,2,1,0:T(8,128)(2,1)}), bf16[4,2,2,128,128]{4,3,2,1,0:T(8,128)(2,1)S(1)}, u32[]{:S(2)}, u32[]{:S(2)}) async-start(bf16[4,2,2,128,128]{4,3,2,1,0:T(8,128)(2,1)} %broadcast_select_fusion), calls=%async_computation.1 | async-start | bytes 1048576 | tf_op jit(solution)/shard_map/all_to_all | solution.py:68
  51.8 2.0 %copy-start.1 = (bf16[16,2,2,128,128]{4,3,2,0,1:T(8,128)(2,1)}, bf16[16,2,2,128,128]{4,3,2,0,1:T(8,128)(2,1)S(1)}, u32[]{:S(2)}) copy-start(bf16[16,2,2,128,128]{4,3,2,0,1:T(8,128)(2,1)S(1)} %fusion.4) | copy-start | bytes 6291460
  51.8 2.0 %copy-start.3 = (bf16[16,2,8,128]{3,2,1,0:T(8,128)(2,1)S(1)}, bf16[16,2,8,128]{3,2,1,0:T(8,128)(2,1)}, u32[]{:S(2)}) copy-start(bf16[16,2,8,128]{3,2,1,0:T(8,128)(2,1)} %param.11) | copy-start | bytes 196612
where the time goes:
time: 75.1 us; the launch traced here: 74.6 us
  local copies, waits for them, and re-layouts  19.9 us (26%)
  blocking collectives  13.5 us (18%)
  waiting for transfers between devices  12.8 us (17%)
  starting transfers between devices  11.4 us (15%)
  other arithmetic  9.31 us (12%)
  matrix products  6.29 us (8%)
  between operations  1.44 us (2%)
    unnamed x1, blocking collectives  13.5 us
    all_to_all x1, waiting for transfers between devices, body(): lax.all_to_all(outbox, 'inst', split_axis=0, concat_axis=0, tiled=True)  12.8 us
    all_to_all x1, starting transfers between devices, body(): lax.all_to_all(out_len.astype(jnp.bfloat16), 'inst', split_axis=0, concat...  6.32 us
    all_to_all x1, starting transfers between devices, body(): lax.all_to_all(outbox, 'inst', split_axis=0, concat_axis=0, tiled=True)  5.1 us
    gather x1, local copies, waits for them, and re-layouts, body(): home = mine[partner_slot]  3.77 us
    dot_general x1, matrix products, body(): product = jnp.dot(flattened, out_weight, preferred_element_type=jnp.float32)  3.48 us
    select_n x1, other arithmetic, append_tokens(): jnp.where(landing[:, None, None, :, None], fresh[:, step][:, :, :, None,...  3.47 us
    unnamed x13, local copies, waits for them, and re-layouts  3.28 us
  transfers between devices with their start and end apart: 2, of which 1 were waited for; matrix products, arithmetic and copies ran while one was open for 24% of the time, Pallas kernels for 0%

commit v1 on v0

v1 whole, which is shorter than its diff:
```python
import functools

import jax
import jax.numpy as jnp
from jax import lax
from jax.experimental import pallas as pl
from jax.experimental.pallas import tpu as pltpu
from jax.sharding import PartitionSpec as P

MESH = pl.DeviceIdType.MESH
BF16 = jnp.bfloat16
F32 = jnp.float32
WIDE = 512


def move_kernel(
    dims, pt, ln, pr, q_ref, nk_ref, pool_hbm, w_hbm, loc_hbm, arr_hbm, lo_ref,
    poolv, wv, qn, qbox, qarr, obox, locv, att, abox, aarr, merged, flat, prodf, pbox, parr,
    dma_sem, loc_sem, q_send, q_recv, p_send, p_recv, a_send, a_recv, r_send, r_recv,
):
    n, tp, slots, steps, heads, groups, pages, page, span, hd, features = dims
    rows = steps * heads
    new_at = -(-rows // 16) * 16
    per = heads // groups
    body = 2 * groups * span
    me = lax.axis_index("inst")
    col = lax.axis_index("tp")
    own = slots // tp * steps
    fold = max(1, 16 // own)
    narrow = WIDE // fold
    chunks = features // WIDE

    pool_copy = pltpu.make_async_copy(pool_hbm, poolv, dma_sem.at[0])
    pool_copy.start()
    w_copy = pltpu.make_async_copy(w_hbm, wv, dma_sem.at[1])
    w_copy.start()

    barrier = pltpu.get_barrier_semaphore()
    for k in range(1, n):
        pl.semaphore_signal(
            barrier, inc=1, device_id={"inst": lax.rem(me + k, n)}, device_id_type=MESH
        )
    for i in range(1, tp):
        pl.semaphore_signal(
            barrier, inc=1, device_id={"tp": lax.rem(col + i, tp)}, device_id_type=MESH
        )

    def pack(j, carry):
        parts = [q_ref[j, t].astype(F32) for t in range(steps)]
        if new_at > rows:
            parts.append(jnp.zeros((new_at - rows, hd), F32))
        parts += [nk_ref[j, t, c].astype(F32) for t in range(steps) for c in range(2)]
        fill = qn.shape[1] - new_at - steps * 2 * groups
        parts.append(jnp.zeros((fill, hd), F32))
        qn[j] = jnp.concatenate(parts, axis=0).astype(BF16)
        return carry

    lax.fori_loop(0, slots, pack, 0)

    def slot_for(k):
        other = lax.rem(me + k, n)
        found = jnp.int32(0)
        for j in range(slots):
            found = jnp.where(pr[j] // slots == other, jnp.int32(j), found)
        return found

    def build_q(k, carry):
        qbox[k] = qn[slot_for(k)]
        return carry

    lax.fori_loop(1, n, build_q, 0)
    aarr[0] = jnp.zeros(aarr.shape[1:], BF16)
    pl.semaphore_wait(barrier, n - 1 + tp - 1)

    def remote(src, dst, send, recv, where):
        return pltpu.make_async_remote_copy(
            src_ref=src, dst_ref=dst, send_sem=send, recv_sem=recv,
            device_id=where, device_id_type=MESH,
        )

    def q_copy(k):
        return remote(qbox.at[k], qarr.at[k], q_send.at[k], q_recv.at[k],
                      {"inst": lax.rem(me + k, n)})

    def p_copy(k):
        return remote(obox.at[k], arr_hbm.at[k], p_send.at[k], p_recv.at[k],
                      {"inst": lax.rem(me + k, n)})

    def a_copy(k):
        return remote(abox.at[k], aarr.at[k], a_send.at[k], a_recv.at[k],
                      {"inst": lax.rem(me + k, n)})

    order = sorted(range(1, n), key=lambda k: abs(k - n // 2))
    for k in order:
        q_copy(k).start()
    pool_copy.wait()

    row_at = lax.broadcasted_iota(jnp.int32, (page, hd), 0)

    def stored(slot, known):
        for m in range(pages):
            at = row_at + page * m
            inside = at < known
            where = pt[slot, m]
            for c in range(2):
                for g in range(groups):
                    x = poolv[where, c, g].astype(F32)
                    yield m, c, g, at, jnp.where(inside, x, 0.0)

    def place(m, c, g):
        return pl.ds((c * groups + g) * span + page * m, page)

    def build_pages(k):
        slot = slot_for(k)
        known = ln[slot]
        for m, c, g, _, x in stored(slot, known):
            obox[k, place(m, c, g), :] = x.astype(BF16)
        obox[k, pl.ds(body, 16), :] = jnp.full((16, hd), known.astype(F32), F32).astype(BF16)

    for k in order:
        build_pages(k)
        p_copy(k).start()

    def fresh_rows(packed):
        extra = packed[new_at:].astype(F32)
        return lambda t, c, g: extra[(t * 2 + c) * groups + g:(t * 2 + c) * groups + g + 1]

    r_at = lax.broadcasted_iota(jnp.int32, (rows, groups * span), 0)
    c_at = lax.broadcasted_iota(jnp.int32, (rows, groups * span), 1)
    same = (r_at % heads) // per == c_at // span
    ahead = c_at % span - r_at // heads

    def attend(asked, keys, values, known):
        scores = lax.dot_general(
            asked, keys, (((1,), (1,)), ((), ())), preferred_element_type=F32
        ) * (hd ** -0.5)
        scores = jnp.where(same & (ahead <= known), scores, -1e30)
        expo = jnp.exp(scores - jnp.max(scores, axis=-1, keepdims=True))
        weights = (expo / jnp.sum(expo, axis=-1, keepdims=True)).astype(BF16)
        return jnp.dot(weights, values, preferred_element_type=F32)

    def finish(slot, known, packed, dst, j):
        new = fresh_rows(packed)
        for m, c, g, at, x in stored(slot, known):
            for t in range(steps):
                x = jnp.where(at == known + t, new(t, c, g), x)
            dst[j, place(m, c, g), :] = x.astype(BF16)

    half = groups * span
    extra = slots

    def leaver(k):
        slot = slot_for(k)
        known = ln[slot]
        packed = qarr[n - k]
        finish(slot, known, packed, locv, extra)
        out = attend(packed[:rows], locv[extra, pl.ds(0, half), :],
                     locv[extra, pl.ds(half, half), :], known)
        if rows < 16:
            out = jnp.concatenate([out, jnp.zeros((16 - rows, hd), F32)], axis=0)
        abox[k] = out.astype(BF16)

    for k in order:
        q_copy(n - k).wait_recv()
        leaver(k)
        a_copy(k).start()

    def stay(j, carry):
        slot = pr[j] % slots
        known = ln[slot]
        packed = qn[j]
        finish(slot, known, packed, locv, j)
        pltpu.make_async_copy(locv.at[j], loc_hbm.at[j], loc_sem.at[j]).start()
        att[j] = attend(packed[:rows], locv[j, pl.ds(0, half), :],
                        locv[j, pl.ds(half, half), :], known)
        return carry

    lax.fori_loop(0, slots, stay, 0, unroll=4)

    for k in order:
        a_copy(k).wait_recv()
    for j in range(slots):
        back = lax.rem(me - pr[j] // slots + n, n)
        got = aarr[back].astype(F32)[:rows]
        merged[pl.ds(j * rows, rows), :] = jnp.where(back == 0, att[j], got)
    for h in range(heads):
        flat[:, pl.ds(h * hd, hd)] = merged[
            pl.ds(h, slots * steps, stride=heads), :
        ].astype(BF16)
    w_copy.wait()

    def r_copy(c, i):
        return remote(pbox.at[c, lax.rem(col + i, tp)], parr.at[c, i], r_send.at[c, i],
                      r_recv.at[c, i], {"tp": lax.rem(col + i, tp)})

    for c in range(chunks):
        prod = jnp.dot(flat[...], wv[:, pl.ds(c * WIDE, WIDE)], preferred_element_type=F32)
        for d in range(tp):
            mine = prod[d * own:(d + 1) * own]
            prodf[c, d] = mine
            pbox[c, d] = jnp.concatenate(
                [mine[:, f * narrow:(f + 1) * narrow] for f in range(fold)], axis=0
            ).astype(BF16)
        for i in range(1, tp):
            r_copy(c, i).start()
    for c in range(chunks):
        total = prodf[c, col]
        for i in range(1, tp):
            r_copy(c, i).wait_recv()
            part = parr[c, i].astype(F32)
            total += jnp.concatenate(
                [part[f * own:(f + 1) * own] for f in range(fold)], axis=1
            )
        for r in range(own // steps):
            lo_ref[r, :, pl.ds(c * WIDE, WIDE)] = total[r * steps:(r + 1) * steps].astype(BF16)

    for c in range(chunks):
        for i in range(1, tp):
            r_copy(c, i).wait_send()
    for k in order:
        q_copy(k).wait_send()
        a_copy(k).wait_send()
    for j in range(slots):
        pltpu.make_async_copy(locv.at[j], loc_hbm.at[j], loc_sem.at[j]).wait()
    for k in order:
        p_copy(k).wait_send()
        p_copy(k).wait_recv()


def place_kernel(dims, pr, nk_ref, loc_hbm, arr_hbm, lo_in, new_hbm, lo_out, vbuf, sem, in_sem):
    n, tp, slots, steps, heads, groups, pages, page, span, hd, features = dims
    body = 2 * groups * span
    me = lax.axis_index("inst")
    lo_copy = pltpu.make_async_copy(lo_in, lo_out, sem.at[slots])
    lo_copy.start()

    def source(j):
        return lax.rem(me - pr[j] // slots + n, n)

    def fetch(j):
        return pltpu.make_async_copy(arr_hbm.at[source(j)], vbuf.at[source(j)], in_sem.at[j])

    def keep(j):
        return pltpu.make_async_copy(loc_hbm.at[j], new_hbm.at[j], sem.at[j])

    def put(j):
        return pltpu.make_async_copy(vbuf.at[source(j), pl.ds(0, body)], new_hbm.at[j], sem.at[j])

    for j in range(slots):
        moved = source(j) != 0

        @pl.when(moved)
        def _():
            fetch(j).start()

        @pl.when(jnp.logical_not(moved))
        def _():
            keep(j).start()

    at = lax.broadcasted_iota(jnp.int32, (span, hd), 0)
    for j in range(slots):
        @pl.when(source(j) != 0)
        def _():
            fetch(j).wait()
            k = source(j)
            known = vbuf[k, pl.ds(body, 16), :].astype(F32)[:1].astype(jnp.int32)
            for c in range(2):
                rows = [nk_ref[j, t, c].astype(F32) for t in range(steps)]
                for g in range(groups):
                    where = pl.ds((c * groups + g) * span, span)
                    x = vbuf[k, where, :].astype(F32)
                    for t in range(steps):
                        x = jnp.where(at == known + t, rows[t][g:g + 1], x)
                    vbuf[k, where, :] = x.astype(BF16)
            put(j).start()

    for j in range(slots):
        keep(j).wait()
    lo_copy.wait()


def body(mesh, kv_pool, page_table, lengths, partner, queries, new_kv, out_weight):
    n, tp = mesh.shape["inst"], mesh.shape["tp"]
    slots, steps, heads, hd = queries.shape
    groups, page = kv_pool.shape[2], kv_pool.shape[3]
    pages = page_table.shape[1]
    features = out_weight.shape[1]
    span = pages * page
    dims = (n, tp, slots, steps, heads, groups, pages, page, span, hd, features)
    rows = steps * heads
    up = lambda x: -(-x // 16) * 16
    qrows = up(rows) + up(steps * 2 * groups)
    tokens = 2 * groups * span
    own = slots // tp * steps
    fold = max(1, 16 // own)
    chunks = features // WIDE
    vmem = pl.BlockSpec(memory_space=pltpu.VMEM)
    smem = pl.BlockSpec(memory_space=pltpu.SMEM)
    hbm = pl.BlockSpec(memory_space=pl.ANY)
    dma = pltpu.SemaphoreType.DMA
    loc, arr, lo = pl.pallas_call(
        functools.partial(move_kernel, dims),
        out_shape=(
            jax.ShapeDtypeStruct((slots, tokens, hd), BF16),
            jax.ShapeDtypeStruct((n, tokens + 16, hd), BF16),
            jax.ShapeDtypeStruct((slots // tp, steps, features), BF16),
        ),
        in_specs=[smem, smem, smem, vmem, vmem, hbm, hbm],
        out_specs=(hbm, hbm, vmem),
        scratch_shapes=[
            pltpu.VMEM(kv_pool.shape, BF16),
            pltpu.VMEM(out_weight.shape, BF16),
            pltpu.VMEM((slots, qrows, hd), BF16),
            pltpu.VMEM((n, qrows, hd), BF16),
            pltpu.VMEM((n, qrows, hd), BF16),
            pltpu.VMEM((n, tokens + 16, hd), BF16),
            pltpu.VMEM((slots + 1, tokens, hd), BF16),
            pltpu.VMEM((slots, rows, hd), F32),
            pltpu.VMEM((n, up(rows), hd), BF16),
            pltpu.VMEM((n, up(rows), hd), BF16),
            pltpu.VMEM((slots * rows, hd), F32),
            pltpu.VMEM((slots * steps, heads * hd), BF16),
            pltpu.VMEM((chunks, tp, own, WIDE), F32),
            pltpu.VMEM((chunks, tp, own * fold, WIDE // fold), BF16),
            pltpu.VMEM((chunks, tp, own * fold, WIDE // fold), BF16),
            dma((2,)), dma((slots,)),
            dma((n,)), dma((n,)), dma((n,)), dma((n,)), dma((n,)), dma((n,)),
            dma((chunks, tp)), dma((chunks, tp)),
        ],
        compiler_params=pltpu.CompilerParams(
            collective_id=0, has_side_effects=True, vmem_limit_bytes=28 << 20
        ),
        name="move",
    )(page_table, lengths, partner, queries, new_kv, kv_pool, out_weight)
    new_cache, layer_out = pl.pallas_call(
        functools.partial(place_kernel, dims),
        out_shape=(
            jax.ShapeDtypeStruct((slots, tokens, hd), BF16),
            jax.ShapeDtypeStruct(lo.shape, BF16),
        ),
        in_specs=[smem, vmem, hbm, hbm, hbm],
        out_specs=(hbm, hbm),
        scratch_shapes=[
            pltpu.VMEM((n, tokens + 16, hd), BF16),
            dma((slots + 1,)), dma((slots,)),
        ],
        compiler_params=pltpu.CompilerParams(vmem_limit_bytes=16 << 20),
        name="place",
    )(partner, new_kv, loc, arr, lo)
    return layer_out, new_cache.reshape(slots, 2, groups, span, hd)


def solution(mesh):
    in_specs = (
        P(("groups", "inst"), None, "tp", None, None),
        P(("groups", "inst"), None),
        P(("groups", "inst")),
        P(("groups", "inst")),
        P(("groups", "inst"), None, "tp", None),
        P(("groups", "inst"), None, None, "tp", None),
        P("tp", None),
    )
    out_specs = (
        P(("groups", "inst", "tp"), None, None),
        P(("groups", "inst"), None, "tp", None, None),
    )
    return jax.shard_map(
        functools.partial(body, mesh), mesh=mesh, in_specs=in_specs, out_specs=out_specs,
        check_vma=False,
    )
```

time: 75.1 us -> 41.5 us (0.55)
  Pallas kernels: 0 us -> 32.8 us
  blocking collectives: 13.5 us -> 0 us
  waiting for transfers between devices: 12.8 us -> 0 us
  local copies, waits for them, and re-layouts: 19.9 us -> 7.74 us
  starting transfers between devices: 11.4 us -> 0 us
  other arithmetic: 9.31 us -> 0 us
  matrix products: 6.29 us -> 0 us
  between operations: 1.44 us -> 0.64 us
    pallas_call x0 -> x2, Pallas kernels: none -> 32.8 us  [the longest x1 30.2 us: body(): pl.pallas_call(functools.partial(move_kernel, dims), out_shape=(jax.Shape...]
    gather x7 -> x0, local copies, waits for them, and re-layouts: 13.5 us -> none  [the longest x1 3.77 us: body(): home = mine[partner_slot]]
    unnamed x1 -> x0, blocking collectives: 13.5 us -> none
    all_to_all x2 -> x0, waiting for transfers between devices: 12.8 us -> none  [the longest x1 12.8 us: body(): lax.all_to_all(outbox, 'inst', split_axis=0, concat_axis=0, tiled=True)]
    all_to_all x2 -> x0, starting transfers between devices: 11.4 us -> none  [the longest x1 6.32 us: body(): lax.all_to_all(out_len.astype(jnp.bfloat16), 'inst', split_axis=0, concat...]
    select_n x6 -> x0, other arithmetic: 7.56 us -> none  [the longest x1 3.47 us: append_tokens(): jnp.where(landing[:, None, None, :, None], fresh[:, step][:, :, :, None,...]
    dot_general x3 -> x0, matrix products: 6.29 us -> none  [the longest x1 3.48 us: body(): product = jnp.dot(flattened, out_weight, preferred_element_type=jnp.float32)]
    unnamed x13, local copies, waits for them, and re-layouts: 3.28 us -> 7.74 us
  transfers between devices with their start and end apart: 2 -> 0, of which waited for: 1 -> 0; matrix products, arithmetic and copies ran while one was open for 24% -> 0% of each run, Pallas kernels for 0% -> 0%
where the time goes in v1:
time: 41.5 us; the launch traced here: 41.2 us
  Pallas kernels  32.8 us (79%)
  local copies, waits for them, and re-layouts  7.74 us (19%)
  between operations  0.64 us (2%)
    pallas_call x1, Pallas kernels, body(): pl.pallas_call(functools.partial(move_kernel, dims), out_shape=(jax.Shape...  30.2 us
    unnamed x13, local copies, waits for them, and re-layouts  7.74 us
    pallas_call x1, Pallas kernels, body(): pl.pallas_call(functools.partial(place_kernel, dims), out_shape=(jax.Shap...  2.57 us

profile of v1, /device:TPU:0, one launch (start us, length us, event | category | flops | bytes accessed | tf_op | source)
XLA Modules:
  0.0 41.2 jit_solution(6846447808357892139)
XLA Ops:
  0.6 0.8 %copy.9.pt = s32[16,4]{1,0:T(8,128)S(1)} copy(s32[16,4]{0,1:T(4,128)} %param.8) | data formatting | bytes 512 | tf_op args[1]
  1.4 0.0 copy-start
  1.4 2.5 %copy-done = bf16[1024,2560]{1,0:T(8,128)(2,1)S(1)} copy-done((bf16[1024,2560]{1,0:T(8,128)(2,1)S(1)}, bf16[1024,2560]{1,0:T(8,128)(2,1)}, u32[]{:S(2)}) %copy-start) | copy-done | bytes 5242904
  3.9 0.0 copy-start.1
  3.9 1.6 %copy-done.1 = bf16[64,2,2,32,128]{4,3,2,1,0:T(8,128)(2,1)S(1)} copy-done((bf16[64,2,2,32,128]{4,3,2,1,0:T(8,128)(2,1)S(1)}, bf16[64,2,2,32,128]{4,3,2,1,0:T(8,128)(2,1)}, u32[]{:S(2)}) %copy-start.1) | copy-done | bytes 2097176
  5.5 0.0 copy-start.2
  5.5 0.8 %copy-done.2 = bf16[16,2,2,2,128]{4,3,2,1,0:T(2,128)(2,1)S(1)} copy-done((bf16[16,2,2,2,128]{4,3,2,1,0:T(2,128)(2,1)S(1)}, bf16[16,2,2,2,128]{4,3,2,1,0:T(2,128)(2,1)}, u32[]{:S(2)}) %copy-start.2) | copy-done | bytes 32792
  6.2 0.0 copy-start.3
  6.2 0.8 %copy-done.3 = bf16[16,2,8,128]{3,2,1,0:T(8,128)(2,1)S(1)} copy-done((bf16[16,2,8,128]{3,2,1,0:T(8,128)(2,1)S(1)}, bf16[16,2,8,128]{3,2,1,0:T(8,128)(2,1)}, u32[]{:S(2)}) %copy-start.3) | copy-done | bytes 65560
  7.1 0.0 copy-start.4
  7.1 0.7 %copy-done.4 = s32[16]{0:T(128)S(1)} copy-done((s32[16]{0:T(128)S(1)}, s32[16]{0:T(128)}, u32[]{:S(2)}) %copy-start.4) | copy-done | bytes 88
  7.7 0.0 copy-start.5
  7.7 0.7 %copy-done.5 = s32[16]{0:T(128)S(1)} copy-done((s32[16]{0:T(128)S(1)}, s32[16]{0:T(128)}, u32[]{:S(2)}) %copy-start.5) | copy-done | bytes 88
  8.4 30.2 %move.1 = (bf16[16,512,128]{2,1,0:T(8,128)(2,1)S(1)}, bf16[4,528,128]{2,1,0:T(8,128)(2,1)S(1)}, bf16[4,2,2560]{2,1,0:T(2,128)(2,1)S(1)}) custom-call(s32[16,4]{1,0:T(8,128)S(1)} %copy.9.pt, s32[16]{0:T(128)S(1)} %copy-done.5, s32[16]{0:T(128)S(1)} %copy-done.4, bf16[16,2,8,128]{3,2,1,0:T(8,128)(2,1)S(1)} %copy-done.3, ...), custom_call_target="tpu_custom_call" | custom-call | tf_op jit(solution)/shard_map/move/pallas_call | solution.py:301
  38.6 2.6 %place.1 = (bf16[16,512,128]{2,1,0:T(8,128)(2,1)}, bf16[4,2,2560]{2,1,0:T(2,128)(2,1)}) custom-call(s32[16]{0:T(128)S(1)} %copy-done.4, bf16[16,2,2,2,128]{4,3,2,1,0:T(2,128)(2,1)S(1)} %copy-done.2, bf16[16,512,128]{2,1,0:T(8,128)(2,1)S(1)} %get-tuple-element.7.loc_hbm, bf16[4,528,128]{2,1,0:T(8,128)(2,1)S(1)} %get-tuple-element.8.arr_hbm, ...), custom_call_target="tpu_custom_call" | custom-call | tf_op jit(solution)/shard_map/place/pallas_call | solution.py:335
Async XLA Ops:
  1.4 2.5 %copy-start = (bf16[1024,2560]{1,0:T(8,128)(2,1)S(1)}, bf16[1024,2560]{1,0:T(8,128)(2,1)}, u32[]{:S(2)}) copy-start(bf16[1024,2560]{1,0:T(8,128)(2,1)} %w_hbm.1) | copy-start | bytes 15728644
  3.9 1.6 %copy-start.1 = (bf16[64,2,2,32,128]{4,3,2,1,0:T(8,128)(2,1)S(1)}, bf16[64,2,2,32,128]{4,3,2,1,0:T(8,128)(2,1)}, u32[]{:S(2)}) copy-start(bf16[64,2,2,32,128]{4,3,2,1,0:T(8,128)(2,1)} %pool_hbm.1) | copy-start | bytes 6291460
  5.5 0.8 %copy-start.2 = (bf16[16,2,2,2,128]{4,3,2,1,0:T(2,128)(2,1)S(1)}, bf16[16,2,2,2,128]{4,3,2,1,0:T(2,128)(2,1)}, u32[]{:S(2)}) copy-start(bf16[16,2,2,2,128]{4,3,2,1,0:T(2,128)(2,1)} %nk_ref.3) | copy-start | bytes 98308
  6.2 0.8 %copy-start.3 = (bf16[16,2,8,128]{3,2,1,0:T(8,128)(2,1)S(1)}, bf16[16,2,8,128]{3,2,1,0:T(8,128)(2,1)}, u32[]{:S(2)}) copy-start(bf16[16,2,8,128]{3,2,1,0:T(8,128)(2,1)} %q_ref.1) | copy-start | bytes 196612
  7.1 0.7 %copy-start.4 = (s32[16]{0:T(128)S(1)}, s32[16]{0:T(128)}, u32[]{:S(2)}) copy-start(s32[16]{0:T(128)} %pr.3) | copy-start | bytes 196
  7.7 0.7 %copy-start.5 = (s32[16]{0:T(128)S(1)}, s32[16]{0:T(128)}, u32[]{:S(2)}) copy-start(s32[16]{0:T(128)} %ln.1) | copy-start | bytes 196

commit v2 on v1

v2 whole, which is shorter than its diff:
```python
import functools

import jax
import jax.numpy as jnp
from jax import lax
from jax.experimental import pallas as pl
from jax.experimental.pallas import tpu as pltpu
from jax.sharding import PartitionSpec as P

MESH = pl.DeviceIdType.MESH
BF16 = jnp.bfloat16
F32 = jnp.float32
WIDE = 512
FIRST = 3
EARLY = 0


def move_kernel(
    dims, pt_hbm, ln_hbm, pr_hbm, q_hbm, nk_hbm, pool_hbm, w_hbm, loc_hbm, arr_hbm, lo_ref,
    pt, ln, pr, q_ref, nk_ref, poolv, wv, qn, qbox, qarr, obox, lbox, locv, att, abox, aarr, merged, flat, prodf, pbox, parr,
    dma_sem, loc_sem, q_send, q_recv, p_send, p_recv, a_send, a_recv, r_send, r_recv,
):
    n, tp, slots, steps, heads, groups, pages, page, span, hd, features = dims
    rows = steps * heads
    new_at = -(-rows // 16) * 16
    per = heads // groups
    body = 2 * groups * span
    me = lax.axis_index("inst")
    col = lax.axis_index("tp")
    own = slots // tp * steps
    fold = max(1, 16 // own)
    narrow = WIDE // fold
    chunks = features // WIDE

    early = [
        pltpu.make_async_copy(src, dst, dma_sem.at[at])
        for at, (src, dst) in enumerate(
            [(pr_hbm, pr), (q_hbm, q_ref), (nk_hbm, nk_ref), (pt_hbm, pt), (ln_hbm, ln)]
        )
    ]
    for copy in early:
        copy.start()
    pool_copy = pltpu.make_async_copy(pool_hbm, poolv, dma_sem.at[5])
    pool_copy.start()
    w_copy = pltpu.make_async_copy(w_hbm, wv, dma_sem.at[6])

    barrier = pltpu.get_barrier_semaphore()
    for k in range(1, n):
        pl.semaphore_signal(
            barrier, inc=1, device_id={"inst": lax.rem(me + k, n)}, device_id_type=MESH
        )
    for i in range(1, tp):
        pl.semaphore_signal(
            barrier, inc=1, device_id={"tp": lax.rem(col + i, tp)}, device_id_type=MESH
        )

    for copy in early:
        copy.wait()
    aarr[0] = jnp.zeros(aarr.shape[1:], BF16)

    def slot_for(k):
        other = lax.rem(me + k, n)
        found = jnp.int32(0)
        for j in range(slots):
            found = jnp.where(pr[j] // slots == other, jnp.int32(j), found)
        return found

    def pack(j):
        parts = [q_ref[j, t].astype(F32) for t in range(steps)]
        if new_at > rows:
            parts.append(jnp.zeros((new_at - rows, hd), F32))
        parts += [nk_ref[j, t, c].astype(F32) for t in range(steps) for c in range(2)]
        fill = qn.shape[1] - new_at - steps * 2 * groups
        parts.append(jnp.zeros((fill, hd), F32))
        return jnp.concatenate(parts, axis=0).astype(BF16)

    order = sorted(range(1, n), key=lambda k: abs(k - n // 2))
    leaving = {k: slot_for(k) for k in order}
    for k in order:
        qbox[k] = pack(leaving[k])

    def remote(src, dst, send, recv, where):
        return pltpu.make_async_remote_copy(
            src_ref=src, dst_ref=dst, send_sem=send, recv_sem=recv,
            device_id=where, device_id_type=MESH,
        )

    def q_copy(k):
        return remote(qbox.at[k], qarr.at[k], q_send.at[k], q_recv.at[k],
                      {"inst": lax.rem(me + k, n)})

    cut = (body + 16) // FIRST // 16 * 16

    def p_copy(k, part):
        at = pl.ds(0, cut) if part == 0 else pl.ds(cut, body + 16 - cut)
        return remote(obox.at[k, at], arr_hbm.at[k, at], p_send.at[k, part],
                      p_recv.at[k, part], {"inst": lax.rem(me + k, n)})

    def a_copy(k):
        return remote(abox.at[k], aarr.at[k], a_send.at[k], a_recv.at[k],
                      {"inst": lax.rem(me + k, n)})

    row_at = lax.broadcasted_iota(jnp.int32, (page, hd), 0)

    def stored(slot, known):
        for m in range(pages):
            at = row_at + page * m
            inside = at < known
            where = pt[m, slot]
            for c in range(2):
                for g in range(groups):
                    x = poolv[where, c, g].astype(F32)
                    yield m, c, g, at, jnp.where(inside, x, 0.0)

    def place(m, c, g):
        return pl.ds((c * groups + g) * span + page * m, page)

    pl.semaphore_wait(barrier, n - 1 + tp - 1)
    for k in order:
        q_copy(k).start()
    pool_copy.wait()
    w_copy.start()
    for k in order:
        known = ln[leaving[k]]
        for m, c, g, _, x in stored(leaving[k], known):
            obox[k, place(m, c, g), :] = x.astype(BF16)
        obox[k, pl.ds(body, 16), :] = jnp.full((16, hd), known.astype(F32), F32).astype(BF16)
        p_copy(k, 0).start()

    r_at = lax.broadcasted_iota(jnp.int32, (rows, groups * span), 0)
    c_at = lax.broadcasted_iota(jnp.int32, (rows, groups * span), 1)
    same = (r_at % heads) // per == c_at // span
    ahead = c_at % span - r_at // heads
    reach = jnp.where(same, ahead, span * 2)
    half = groups * span

    def finish(slot, packed, dst, j):
        known = ln[slot]
        new = packed[new_at:].astype(F32)
        for m, c, g, at, x in stored(slot, known):
            for t in range(steps):
                r = (t * 2 + c) * groups + g
                x = jnp.where(at == known + t, new[r:r + 1], x)
            dst[j, place(m, c, g), :] = x.astype(BF16)

    def attend(asked, kept, knowns):
        scores = [
            jnp.where(
                reach <= known,
                lax.dot_general(
                    q, ref[at, pl.ds(0, half), :], (((1,), (1,)), ((), ())),
                    preferred_element_type=F32,
                ) * (hd ** -0.5),
                -1e30,
            )
            for q, (ref, at), known in zip(asked, kept, knowns)
        ]
        scores = jnp.concatenate(scores, axis=0)
        expo = jnp.exp(scores - jnp.max(scores, axis=-1, keepdims=True))
        weights = expo / jnp.sum(expo, axis=-1, keepdims=True)
        return [
            jnp.dot(weights[i * rows:(i + 1) * rows].astype(BF16),
                    ref[at, pl.ds(half, half), :], preferred_element_type=F32)
            for i, (ref, at) in enumerate(kept)
        ]

    def stays(low, high):
        def one(j, carry):
            packed = pack(j)
            qn[j] = packed
            finish(pr[j] % slots, packed, locv, j)
            pltpu.make_async_copy(locv.at[j], loc_hbm.at[j], loc_sem.at[j]).start()
            return carry

        lax.fori_loop(low, high, one, 0, unroll=2)
        js = range(low, high)
        outs = attend([qn[j, pl.ds(0, new_at), :][:rows] for j in js], [(locv, j) for j in js],
                      [ln[pr[j] % slots] for j in js])
        for j, out in zip(js, outs):
            att[j] = out

    early_slots = slots // EARLY if EARLY else 0
    if early_slots:
        stays(0, early_slots)
    for k in order:
        q_copy(n - k).wait_recv()
        finish(leaving[k], qarr[n - k], lbox, k)
    outs = attend([qarr[n - k, pl.ds(0, new_at), :][:rows] for k in order],
                  [(lbox, k) for k in order], [ln[leaving[k]] for k in order])
    for k, out in zip(order, outs):
        if rows < 16:
            out = jnp.concatenate([out, jnp.zeros((16 - rows, hd), F32)], axis=0)
        abox[k] = out.astype(BF16)
        a_copy(k).start()
    for k in order:
        p_copy(k, 1).start()
    stays(early_slots, slots)

    for k in order:
        a_copy(k).wait_recv()
    for j in range(slots):
        back = lax.rem(me - pr[j] // slots + n, n)
        got = aarr[back].astype(F32)[:rows]
        merged[pl.ds(j * rows, rows), :] = jnp.where(back == 0, att[j], got)
    for h in range(heads):
        flat[:, pl.ds(h * hd, hd)] = merged[
            pl.ds(h, slots * steps, stride=heads), :
        ].astype(BF16)
    w_copy.wait()

    def r_copy(c, i):
        return remote(pbox.at[c, lax.rem(col + i, tp)], parr.at[c, i], r_send.at[c, i],
                      r_recv.at[c, i], {"tp": lax.rem(col + i, tp)})

    for c in range(chunks):
        prod = jnp.dot(flat[...], wv[:, pl.ds(c * WIDE, WIDE)], preferred_element_type=F32)
        for d in range(tp):
            mine = prod[d * own:(d + 1) * own]
            prodf[c, d] = mine
            pbox[c, d] = jnp.concatenate(
                [mine[:, f * narrow:(f + 1) * narrow] for f in range(fold)], axis=0
            ).astype(BF16)
        for i in range(1, tp):
            r_copy(c, i).start()
    for c in range(chunks):
        total = prodf[c, col]
        for i in range(1, tp):
            r_copy(c, i).wait_recv()
            part = parr[c, i].astype(F32)
            total += jnp.concatenate(
                [part[f * own:(f + 1) * own] for f in range(fold)], axis=1
            )
        for r in range(own // steps):
            lo_ref[r, :, pl.ds(c * WIDE, WIDE)] = total[r * steps:(r + 1) * steps].astype(BF16)

    for c in range(chunks):
        for i in range(1, tp):
            r_copy(c, i).wait_send()
    for k in order:
        q_copy(k).wait_send()
        a_copy(k).wait_send()
    for j in range(slots):
        pltpu.make_async_copy(locv.at[j], loc_hbm.at[j], loc_sem.at[j]).wait()
    for k in order:
        for part in range(2):
            p_copy(k, part).wait_send()
            p_copy(k, part).wait_recv()


def place_kernel(dims, pr, nk_ref, loc_hbm, arr_hbm, lo_in, new_hbm, lo_out, vbuf, sem, in_sem):
    n, tp, slots, steps, heads, groups, pages, page, span, hd, features = dims
    body = 2 * groups * span
    me = lax.axis_index("inst")
    lo_copy = pltpu.make_async_copy(lo_in, lo_out, sem.at[slots])
    lo_copy.start()

    def source(j):
        return lax.rem(me - pr[j] // slots + n, n)

    def arrived(j):
        return pltpu.make_async_copy(arr_hbm.at[source(j)], vbuf.at[j], in_sem.at[j])

    def kept(j):
        return pltpu.make_async_copy(loc_hbm.at[j], vbuf.at[j, pl.ds(0, body)], in_sem.at[j])

    def put(j):
        return pltpu.make_async_copy(vbuf.at[j, pl.ds(0, body)], new_hbm.at[j], sem.at[j])

    for j in range(slots):
        @pl.when(source(j) != 0)
        def _():
            arrived(j).start()

        @pl.when(source(j) == 0)
        def _():
            kept(j).start()

    at = lax.broadcasted_iota(jnp.int32, (span, hd), 0)
    for j in range(slots):
        @pl.when(source(j) == 0)
        def _():
            kept(j).wait()

        @pl.when(source(j) != 0)
        def _():
            arrived(j).wait()
            known = vbuf[j, pl.ds(body, 16), :].astype(F32)[:1].astype(jnp.int32)
            for c in range(2):
                rows = [nk_ref[j, t, c].astype(F32) for t in range(steps)]
                for g in range(groups):
                    where = pl.ds((c * groups + g) * span, span)
                    x = vbuf[j, where, :].astype(F32)
                    for t in range(steps):
                        x = jnp.where(at == known + t, rows[t][g:g + 1], x)
                    vbuf[j, where, :] = x.astype(BF16)

        put(j).start()

    for j in range(slots):
        put(j).wait()
    lo_copy.wait()


def body(mesh, kv_pool, page_table, lengths, partner, queries, new_kv, out_weight):
    n, tp = mesh.shape["inst"], mesh.shape["tp"]
    slots, steps, heads, hd = queries.shape
    groups, page = kv_pool.shape[2], kv_pool.shape[3]
    pages = page_table.shape[1]
    features = out_weight.shape[1]
    span = pages * page
    dims = (n, tp, slots, steps, heads, groups, pages, page, span, hd, features)
    rows = steps * heads
    up = lambda x: -(-x // 16) * 16
    qrows = up(rows) + up(steps * 2 * groups)
    tokens = 2 * groups * span
    own = slots // tp * steps
    fold = max(1, 16 // own)
    chunks = features // WIDE
    vmem = pl.BlockSpec(memory_space=pltpu.VMEM)
    smem = pl.BlockSpec(memory_space=pltpu.SMEM)
    hbm = pl.BlockSpec(memory_space=pl.ANY)
    dma = pltpu.SemaphoreType.DMA
    loc, arr, lo = pl.pallas_call(
        functools.partial(move_kernel, dims),
        out_shape=(
            jax.ShapeDtypeStruct((slots, tokens, hd), BF16),
            jax.ShapeDtypeStruct((n, tokens + 16, hd), BF16),
            jax.ShapeDtypeStruct((slots // tp, steps, features), BF16),
        ),
        in_specs=[hbm] * 7,
        out_specs=(hbm, hbm, vmem),
        scratch_shapes=[
            pltpu.SMEM((pages, slots), jnp.int32),
            pltpu.SMEM((slots,), jnp.int32),
            pltpu.SMEM((slots,), jnp.int32),
            pltpu.VMEM(queries.shape, BF16),
            pltpu.VMEM(new_kv.shape, BF16),
            pltpu.VMEM(kv_pool.shape, BF16),
            pltpu.VMEM(out_weight.shape, BF16),
            pltpu.VMEM((slots, qrows, hd), BF16),
            pltpu.VMEM((n, qrows, hd), BF16),
            pltpu.VMEM((n, qrows, hd), BF16),
            pltpu.VMEM((n, tokens + 16, hd), BF16),
            pltpu.VMEM((n, tokens, hd), BF16),
            pltpu.VMEM((slots, tokens, hd), BF16),
            pltpu.VMEM((slots, rows, hd), F32),
            pltpu.VMEM((n, up(rows), hd), BF16),
            pltpu.VMEM((n, up(rows), hd), BF16),
            pltpu.VMEM((slots * rows, hd), F32),
            pltpu.VMEM((slots * steps, heads * hd), BF16),
            pltpu.VMEM((chunks, tp, own, WIDE), F32),
            pltpu.VMEM((chunks, tp, own * fold, WIDE // fold), BF16),
            pltpu.VMEM((chunks, tp, own * fold, WIDE // fold), BF16),
            dma((7,)), dma((slots,)),
            dma((n,)), dma((n,)), dma((n, 2)), dma((n, 2)), dma((n,)), dma((n,)),
            dma((chunks, tp)), dma((chunks, tp)),
        ],
        compiler_params=pltpu.CompilerParams(
            collective_id=0, has_side_effects=True, vmem_limit_bytes=60 << 20
        ),
        name="move",
    )(page_table.T, lengths, partner, queries, new_kv, kv_pool, out_weight)
    new_cache, layer_out = pl.pallas_call(
        functools.partial(place_kernel, dims),
        out_shape=(
            jax.ShapeDtypeStruct((slots, tokens, hd), BF16),
            jax.ShapeDtypeStruct(lo.shape, BF16),
        ),
        in_specs=[smem, vmem, hbm, hbm, hbm],
        out_specs=(hbm, hbm),
        scratch_shapes=[
            pltpu.VMEM((slots, tokens + 16, hd), BF16),
            dma((slots + 1,)), dma((slots,)),
        ],
        compiler_params=pltpu.CompilerParams(vmem_limit_bytes=60 << 20),
        name="place",
    )(partner, new_kv, loc, arr, lo)
    return layer_out, new_cache.reshape(slots, 2, groups, span, hd)


def solution(mesh):
    in_specs = (
        P(("groups", "inst"), None, "tp", None, None),
        P(("groups", "inst"), None),
        P(("groups", "inst")),
        P(("groups", "inst")),
        P(("groups", "inst"), None, "tp", None),
        P(("groups", "inst"), None, None, "tp", None),
        P("tp", None),
    )
    out_specs = (
        P(("groups", "inst", "tp"), None, None),
        P(("groups", "inst"), None, "tp", None, None),
    )
    return jax.shard_map(
        functools.partial(body, mesh), mesh=mesh, in_specs=in_specs, out_specs=out_specs,
        check_vma=False,
    )
```

time: 41.5 us -> 24.8 us (0.60)
  Pallas kernels: 32.8 us -> 24 us
  local copies, waits for them, and re-layouts: 7.74 us -> 0 us
    pallas_call x1, Pallas kernels: 30.2 us -> 20.5 us  [body(): pl.pallas_call(functools.partial(move_kernel, dims), out_shape=(jax.Shape...]
    unnamed x13 -> x0, local copies, waits for them, and re-layouts: 7.74 us -> none
    pallas_call x1, Pallas kernels: 2.57 us -> 3.46 us  [body(): pl.pallas_call(functools.partial(place_kernel, dims), out_shape=(jax.Shap...]
where the time goes in v2:
time: 24.8 us; the launch traced here: 24.6 us
  Pallas kernels  24 us (97%)
  between operations  0.64 us (3%)
    pallas_call x1, Pallas kernels, body(): pl.pallas_call(functools.partial(move_kernel, dims), out_shape=(jax.Shape...  20.5 us
    pallas_call x1, Pallas kernels, body(): pl.pallas_call(functools.partial(place_kernel, dims), out_shape=(jax.Shap...  3.46 us

profile of v2, /device:TPU:0, one launch (start us, length us, event | category | flops | bytes accessed | tf_op | source)
XLA Modules:
  0.0 24.6 jit_solution(14949387354635085218)
XLA Ops:
  0.6 20.5 %move.1 = (bf16[16,512,128]{2,1,0:T(8,128)(2,1)}, bf16[4,528,128]{2,1,0:T(8,128)(2,1)}, bf16[4,2,2560]{2,1,0:T(2,128)(2,1)}) custom-call(s32[4,16]{1,0:T(4,128)} %bitcast.2, s32[16]{0:T(128)} %ln_hbm.1, s32[16]{0:T(128)} %pr.1, bf16[16,2,8,128]{3,2,1,0:T(8,128)(2,1)} %q_hbm.1, bf16[16,2,2,2,128]{4,3,2,1,0:T(2,128)(2,1)} %nk_ref.1, ...), custom_call_target="tpu_custom_call" | custom-call | tf_op jit(solution)/shard_map/move/pallas_call | solution.py:323
  21.1 3.5 %place.1 = (bf16[16,512,128]{2,1,0:T(8,128)(2,1)}, bf16[4,2,2560]{2,1,0:T(2,128)(2,1)}) custom-call(s32[16]{0:T(128)} %pr.1, bf16[16,2,2,2,128]{4,3,2,1,0:T(2,128)(2,1)} %nk_ref.1, bf16[16,512,128]{2,1,0:T(8,128)(2,1)} %get-tuple-element.7.loc_hbm, bf16[4,528,128]{2,1,0:T(8,128)(2,1)} %get-tuple-element.8.arr_hbm, bf16[4,2,2560]{2,1,0:T(2,128)(2,1)} %get-tuple-element.9.lo_in), custom_call_target="tpu_custom_call" | custom-call | tf_op jit(solution)/shard_map/place/pallas_call | solution.py:363

commit v3 on v2

--- a/solution.py
+++ b/solution.py
@@ -10,9 +10,16 @@
 MESH = pl.DeviceIdType.MESH
 BF16 = jnp.bfloat16
 F32 = jnp.float32
-WIDE = 512
-FIRST = 3
-EARLY = 0
+FIRST = 4
+CH = 2
+EARLY = 4
+
+
+def width(features, fold):
+    parts = CH
+    while features % parts or features // parts % (128 * fold):
+        parts += 1
+    return features // parts
 
 
 def move_kernel(
@@ -29,8 +36,9 @@
     col = lax.axis_index("tp")
     own = slots // tp * steps
     fold = max(1, 16 // own)
-    narrow = WIDE // fold
-    chunks = features // WIDE
+    wide = width(features, fold)
+    narrow = wide // fold
+    chunks = features // wide
 
     early = [
         pltpu.make_async_copy(src, dst, dma_sem.at[at])
@@ -213,7 +221,7 @@
                       r_recv.at[c, i], {"tp": lax.rem(col + i, tp)})
 
     for c in range(chunks):
-        prod = jnp.dot(flat[...], wv[:, pl.ds(c * WIDE, WIDE)], preferred_element_type=F32)
+        prod = jnp.dot(flat[...], wv[:, pl.ds(c * wide, wide)], preferred_element_type=F32)
         for d in range(tp):
             mine = prod[d * own:(d + 1) * own]
             prodf[c, d] = mine
@@ -231,7 +239,7 @@
                 [part[f * own:(f + 1) * own] for f in range(fold)], axis=1
             )
         for r in range(own // steps):
-            lo_ref[r, :, pl.ds(c * WIDE, WIDE)] = total[r * steps:(r + 1) * steps].astype(BF16)
+            lo_ref[r, :, pl.ds(c * wide, wide)] = total[r * steps:(r + 1) * steps].astype(BF16)
 
     for c in range(chunks):
         for i in range(1, tp):
@@ -247,57 +255,64 @@
             p_copy(k, part).wait_recv()
 
 
-def place_kernel(dims, pr, nk_ref, loc_hbm, arr_hbm, lo_in, new_hbm, lo_out, vbuf, sem, in_sem):
+def place_kernel(
+    dims, pr_hbm, nk_hbm, loc_hbm, arr_hbm, lo_in, new_hbm, lo_out,
+    pr, nk_ref, vbuf, abuf, small_sem, put_sem, loc_sem, arr_sem,
+):
     n, tp, slots, steps, heads, groups, pages, page, span, hd, features = dims
     body = 2 * groups * span
     me = lax.axis_index("inst")
-    lo_copy = pltpu.make_async_copy(lo_in, lo_out, sem.at[slots])
+    pr_copy = pltpu.make_async_copy(pr_hbm, pr, small_sem.at[0])
+    nk_copy = pltpu.make_async_copy(nk_hbm, nk_ref, small_sem.at[1])
+    lo_copy = pltpu.make_async_copy(lo_in, lo_out, small_sem.at[2])
+
+    def arrived(k):
+        return pltpu.make_async_copy(arr_hbm.at[k], abuf.at[k], arr_sem.at[k])
+
+    def kept(j):
+        return pltpu.make_async_copy(loc_hbm.at[j], vbuf.at[j], loc_sem.at[j])
+
+    pr_copy.start()
+    for k in range(1, n):
+        arrived(k).start()
+    nk_copy.start()
+    for j in range(slots):
+        kept(j).start()
     lo_copy.start()
-
-    def source(j):
-        return lax.rem(me - pr[j] // slots + n, n)
-
-    def arrived(j):
-        return pltpu.make_async_copy(arr_hbm.at[source(j)], vbuf.at[j], in_sem.at[j])
-
-    def kept(j):
-        return pltpu.make_async_copy(loc_hbm.at[j], vbuf.at[j, pl.ds(0, body)], in_sem.at[j])
-
-    def put(j):
-        return pltpu.make_async_copy(vbuf.at[j, pl.ds(0, body)], new_hbm.at[j], sem.at[j])
-
-    for j in range(slots):
-        @pl.when(source(j) != 0)
+    pr_copy.wait()
+    source = [lax.rem(me - pr[j] // slots + n, n) for j in range(slots)]
+
+    def put(j, src):
+        return pltpu.make_async_copy(src, new_hbm.at[j], put_sem.at[j])
+
+    for k in range(1, n):
+        arrived(k).wait()
+    nk_copy.wait()
+    at = lax.broadcasted_iota(jnp.int32, (span, hd), 0)
+    for j in range(slots):
+        @pl.when(source[j] != 0)
         def _():
-            arrived(j).start()
-
-        @pl.when(source(j) == 0)
-        def _():
-            kept(j).start()
-
-    at = lax.broadcasted_iota(jnp.int32, (span, hd), 0)
-    for j in range(slots):
-        @pl.when(source(j) == 0)
-        def _():
-            kept(j).wait()
-
-        @pl.when(source(j) != 0)
-        def _():
-            arrived(j).wait()
-            known = vbuf[j, pl.ds(body, 16), :].astype(F32)[:1].astype(jnp.int32)
+            k = source[j]
+            known = abuf[k, pl.ds(body, 16), :].astype(F32)[:1].astype(jnp.int32)
             for c in range(2):
                 rows = [nk_ref[j, t, c].astype(F32) for t in range(steps)]
                 for g in range(groups):
                     where = pl.ds((c * groups + g) * span, span)
-                    x = vbuf[j, where, :].astype(F32)
+                    x = abuf[k, where, :].astype(F32)
                     for t in range(steps):
                         x = jnp.where(at == known + t, rows[t][g:g + 1], x)
-                    vbuf[j, where, :] = x.astype(BF16)
-
-        put(j).start()
-
-    for j in range(slots):
-        put(j).wait()
+                    abuf[k, where, :] = x.astype(BF16)
+            put(j, abuf.at[k, pl.ds(0, body)]).start()
+
+    for j in range(slots):
+        kept(j).wait()
+
+        @pl.when(source[j] == 0)
+        def _():
+            put(j, vbuf.at[j]).start()
+
+    for j in range(slots):
+        put(j, vbuf.at[j]).wait()
     lo_copy.wait()
 
 
@@ -315,9 +330,9 @@
     tokens = 2 * groups * span
     own = slots // tp * steps
     fold = max(1, 16 // own)
-    chunks = features // WIDE
+    wide = width(features, fold)
+    chunks = features // wide
     vmem = pl.BlockSpec(memory_space=pltpu.VMEM)
-    smem = pl.BlockSpec(memory_space=pltpu.SMEM)
     hbm = pl.BlockSpec(memory_space=pl.ANY)
     dma = pltpu.SemaphoreType.DMA
     loc, arr, lo = pl.pallas_call(
@@ -348,9 +363,9 @@
             pltpu.VMEM((n, up(rows), hd), BF16),
             pltpu.VMEM((slots * rows, hd), F32),
             pltpu.VMEM((slots * steps, heads * hd), BF16),
-            pltpu.VMEM((chunks, tp, own, WIDE), F32),
-            pltpu.VMEM((chunks, tp, own * fold, WIDE // fold), BF16),
-            pltpu.VMEM((chunks, tp, own * fold, WIDE // fold), BF16),
+            pltpu.VMEM((chunks, tp, own, wide), F32),
+            pltpu.VMEM((chunks, tp, own * fold, wide // fold), BF16),
+            pltpu.VMEM((chunks, tp, own * fold, wide // fold), BF16),
             dma((7,)), dma((slots,)),
             dma((n,)), dma((n,)), dma((n, 2)), dma((n, 2)), dma((n,)), dma((n,)),
             dma((chunks, tp)), dma((chunks, tp)),
@@ -366,11 +381,14 @@
             jax.ShapeDtypeStruct((slots, tokens, hd), BF16),
             jax.ShapeDtypeStruct(lo.shape, BF16),
         ),
-        in_specs=[smem, vmem, hbm, hbm, hbm],
+        in_specs=[hbm] * 5,
         out_specs=(hbm, hbm),
         scratch_shapes=[
-            pltpu.VMEM((slots, tokens + 16, hd), BF16),
-            dma((slots + 1,)), dma((slots,)),
+            pltpu.SMEM((slots,), jnp.int32),
+            pltpu.VMEM(new_kv.shape, BF16),
+            pltpu.VMEM((slots, tokens, hd), BF16),
+            pltpu.VMEM((n, tokens + 16, hd), BF16),
+            dma((3,)), dma((slots,)), dma((slots,)), dma((n,)),
         ],
         compiler_params=pltpu.CompilerParams(vmem_limit_bytes=60 << 20),
         name="place",

time: 24.8 us -> 23.7 us (0.956)
  Pallas kernels: 24 us -> 22.9 us
    pallas_call x1, Pallas kernels: 20.5 us -> 19.5 us  [body(): pl.pallas_call(functools.partial(move_kernel, dims), out_shape=(jax.Shape...]
where the time goes in v3:
time: 23.7 us; the launch traced here: 23.6 us
  Pallas kernels  22.9 us (97%)
  between operations  0.64 us (3%)
    pallas_call x1, Pallas kernels, body(): pl.pallas_call(functools.partial(move_kernel, dims), out_shape=(jax.Shape...  19.5 us
    pallas_call x1, Pallas kernels, body(): pl.pallas_call(functools.partial(place_kernel, dims), out_shape=(jax.Shap...  3.43 us

profile of v3, /device:TPU:0, one launch (start us, length us, event | category | flops | bytes accessed | tf_op | source)
XLA Modules:
  0.0 23.6 jit_solution(10481604853589962281)
XLA Ops:
  0.6 19.5 %move.1 = (bf16[16,512,128]{2,1,0:T(8,128)(2,1)}, bf16[4,528,128]{2,1,0:T(8,128)(2,1)}, bf16[4,2,2560]{2,1,0:T(2,128)(2,1)}) custom-call(s32[4,16]{1,0:T(4,128)} %bitcast.2, s32[16]{0:T(128)} %ln_hbm.1, s32[16]{0:T(128)} %pr_hbm.3, bf16[16,2,8,128]{3,2,1,0:T(8,128)(2,1)} %q_hbm.1, bf16[16,2,2,2,128]{4,3,2,1,0:T(2,128)(2,1)} %nk_hbm.3, ...), custom_call_target="tpu_custom_call" | custom-call | tf_op jit(solution)/shard_map/move/pallas_call | solution.py:338
  20.1 3.4 %place.1 = (bf16[16,512,128]{2,1,0:T(8,128)(2,1)}, bf16[4,2,2560]{2,1,0:T(2,128)(2,1)}) custom-call(s32[16]{0:T(128)} %pr_hbm.3, bf16[16,2,2,2,128]{4,3,2,1,0:T(2,128)(2,1)} %nk_hbm.3, bf16[16,512,128]{2,1,0:T(8,128)(2,1)} %get-tuple-element.7.loc_hbm, bf16[4,528,128]{2,1,0:T(8,128)(2,1)} %get-tuple-element.8.arr_hbm, bf16[4,2,2560]{2,1,0:T(2,128)(2,1)} %get-tuple-element.9.lo_in), custom_call_target="tpu_custom_call" | custom-call | tf_op jit(solution)/shard_map/place/pallas_call | solution.py:378

commit v4 on v3

--- a/solution.py
+++ b/solution.py
@@ -82,7 +82,7 @@
         parts.append(jnp.zeros((fill, hd), F32))
         return jnp.concatenate(parts, axis=0).astype(BF16)
 
-    order = sorted(range(1, n), key=lambda k: abs(k - n // 2))
+    order = sorted(range(1, n), key=lambda k: (abs(k - n // 2), -k))
     leaving = {k: slot_for(k) for k in order}
     for k in order:
         qbox[k] = pack(leaving[k])

time: 23.7 us -> 23.4 us (0.987)
  Pallas kernels: 22.9 us -> 22.5 us
    pallas_call x1, Pallas kernels: 19.5 us -> 19.1 us  [body(): pl.pallas_call(functools.partial(move_kernel, dims), out_shape=(jax.Shape...]
where the time goes in v4:
time: 23.4 us; the launch traced here: 23.2 us
  Pallas kernels  22.5 us (96%)
  between operations  0.64 us (3%)
    pallas_call x1, Pallas kernels, body(): pl.pallas_call(functools.partial(move_kernel, dims), out_shape=(jax.Shape...  19.1 us
    pallas_call x1, Pallas kernels, body(): pl.pallas_call(functools.partial(place_kernel, dims), out_shape=(jax.Shap...  3.41 us

profile of v4, /device:TPU:0, one launch (start us, length us, event | category | flops | bytes accessed | tf_op | source)
XLA Modules:
  0.0 23.2 jit_solution(8043970930628223602)
XLA Ops:
  0.6 19.1 %move.1 = (bf16[16,512,128]{2,1,0:T(8,128)(2,1)}, bf16[4,528,128]{2,1,0:T(8,128)(2,1)}, bf16[4,2,2560]{2,1,0:T(2,128)(2,1)}) custom-call(s32[4,16]{1,0:T(4,128)} %bitcast.2, s32[16]{0:T(128)} %ln_hbm.1, s32[16]{0:T(128)} %pr_hbm.3, bf16[16,2,8,128]{3,2,1,0:T(8,128)(2,1)} %q_hbm.1, bf16[16,2,2,2,128]{4,3,2,1,0:T(2,128)(2,1)} %nk_hbm.3, ...), custom_call_target="tpu_custom_call" | custom-call | tf_op jit(solution)/shard_map/move/pallas_call | solution.py:338
  19.8 3.4 %place.1 = (bf16[16,512,128]{2,1,0:T(8,128)(2,1)}, bf16[4,2,2560]{2,1,0:T(2,128)(2,1)}) custom-call(s32[16]{0:T(128)} %pr_hbm.3, bf16[16,2,2,2,128]{4,3,2,1,0:T(2,128)(2,1)} %nk_hbm.3, bf16[16,512,128]{2,1,0:T(8,128)(2,1)} %get-tuple-element.7.loc_hbm, bf16[4,528,128]{2,1,0:T(8,128)(2,1)} %get-tuple-element.8.arr_hbm, bf16[4,2,2560]{2,1,0:T(2,128)(2,1)} %get-tuple-element.9.lo_in), custom_call_target="tpu_custom_call" | custom-call | tf_op jit(solution)/shard_map/place/pallas_call | solution.py:378
